TPU v7x, 32 devices: a whole 2x2x4 slice. The times are simulated.
32 devices in a mesh: groups: 2 (over x), expert: 16 (over z, y, core).
Axes of the slice: x: 2, y: 2, z: 4, core: 2. Of those that a mesh axis runs over, the one named last changes fastest.
Arguments:
- tokens: bfloat16 [4096, 4096], P(('groups', 'expert')), parts along dimension 0, may hold values from -6 to 6
- gate_weight: bfloat16 [16, 4096, 1536], P('expert'), may hold values from -0.09375 to 0.09375
- up_weight: bfloat16 [16, 4096, 1536], P('expert'), may hold values from -0.09375 to 0.09375
- down_weight: bfloat16 [16, 1536, 4096], P('expert'), may hold values from -0.15625 to 0.15625
- expert_ids: int32 [4096, 8], P(('groups', 'expert')), parts along dimension 0, may hold values from 0 to 127, as said below
- slots: int32 [4096, 8], P(('groups', 'expert')), parts along dimension 0, may hold values from -1 to 15, as said below
- gates: float32 [4096, 8], P(('groups', 'expert')), parts along dimension 0, may hold values from 0.25 to 2.5
Outputs:
- mixed: bfloat16 [4096, 4096], P(('groups', 'expert')), parts along dimension 0
There are 2 independent parts, one for each index of `groups`. A program takes and returns all parts, laid end to end along the dimension named above; an argument that names none is the same for every part. Nothing has to cross between parts.
Inputs may be any that keep to these rules, and one draw needn't show every extreme that they name: `expert_ids`: each row names 8 different experts. Only experts 0 to 15 are computed here. Pairs are ranked in the order of rows, then of the 8 choices. A pair has slot -1 if its expert is 16 or above, or if 16 earlier pairs of the rows of the same device name its expert; else its slot is the number of such earlier pairs. So the slots of one expert on one device are 0, 1, ... without gaps. In every draw some expert has all 16 slots filled on every device.
All inputs are finite; a program needn't handle non-finite values.
Results may differ from a plain program's by a relative error of at most 0.0058.
Values may be sent and summed in bfloat16 or wider, within the bound.
A program may use at most 128 MiB of HBM per device.

v0:
```python
import jax
import jax.numpy as jnp
from jax import lax
from jax.sharding import PartitionSpec as P

EXPERTS = 16
CAP = 16


def swiglu_rows(slot_rows, gate_weight, up_weight, down_weight):
    gate_val = jnp.dot(slot_rows, gate_weight[0], preferred_element_type=jnp.float32)
    up_val = jnp.dot(slot_rows, up_weight[0], preferred_element_type=jnp.float32)
    hidden = (jax.nn.silu(gate_val) * up_val).astype(jnp.bfloat16)
    return jnp.dot(hidden, down_weight[0], preferred_element_type=jnp.float32)


def body(tokens, gate_weight, up_weight, down_weight, expert_ids, slots, gates):
    devices = lax.axis_size("expert")
    shards = devices // EXPERTS
    token_count, model_width = tokens.shape
    pair_token = jnp.broadcast_to(
        jnp.arange(token_count, dtype=jnp.int32)[:, None], expert_ids.shape
    )
    filled = slots >= 0
    region = EXPERTS * CAP
    target = jnp.where(filled, expert_ids * CAP + slots, region)
    source_row = (
        jnp.full((region + 1,), token_count, jnp.int32)
        .at[target.reshape(-1)]
        .set(pair_token.reshape(-1))[:region]
    )
    padded = jnp.concatenate([tokens, jnp.zeros((1, model_width), tokens.dtype)], axis=0)
    outgoing = padded[source_row].reshape(EXPERTS, CAP, model_width)
    expert_col = jnp.arange(EXPERTS, dtype=jnp.int32)
    counts = jnp.sum(
        ((expert_ids[:, :, None] == expert_col[None, None, :]) & filled[:, :, None]).astype(
            jnp.int32
        ),
        axis=(0, 1),
    )
    count_send = jnp.repeat(counts, shards).astype(jnp.bfloat16).reshape(devices, 1, 1)
    incoming, arrived = (
        lax.all_to_all(
            jnp.repeat(outgoing, shards, axis=0), "expert", split_axis=0, concat_axis=0, tiled=True
        ),
        lax.all_to_all(count_send, "expert", split_axis=0, concat_axis=0, tiled=True),
    )
    slot_rows = incoming.reshape(devices * CAP, model_width)
    partial_value = swiglu_rows(slot_rows, gate_weight, up_weight, down_weight).astype(jnp.bfloat16)
    returned = lax.all_to_all(
        partial_value.reshape(devices, CAP, model_width),
        "expert",
        split_axis=0,
        concat_axis=0,
        tiled=True,
    )
    expert_out = jnp.sum(
        returned.reshape(EXPERTS, shards, CAP, model_width).astype(jnp.float32), axis=1
    ).reshape(region, model_width)
    combined = jnp.zeros((token_count, model_width), jnp.float32)
    for matrix_lane in range(expert_ids.shape[1]):
        picked = jnp.minimum(target[:, matrix_lane], region - 1)
        combined = combined + jnp.where(
            filled[:, matrix_lane, None], gates[:, matrix_lane, None] * expert_out[picked], 0.0
        )
    return combined.astype(jnp.bfloat16)


def solution(mesh):
    return jax.shard_map(
        body,
        mesh=mesh,
        in_specs=(
            P(("groups", "expert"), None),
            P("expert", None, None),
            P("expert", None, None),
            P("expert", None, None),
            P(("groups", "expert"), None),
            P(("groups", "expert"), None),
            P(("groups", "expert"), None),
        ),
        out_specs=P(("groups", "expert"), None),
        check_vma=False,
    )
```

profile of v0, /device:TPU:16, one launch (start us, length us, event | category | flops | bytes accessed | tf_op | source)
XLA Modules:
  0.0 193.4 jit_solution(1121810243722147026)
XLA Ops:
  0.0 0.7 add_select_fusion
  0.7 0.1 copy.8
  0.8 0.1 reshape.51
  0.9 0.1 reshape.135
  1.0 4.3 %scatter_custom_fusion = s32[257]{0:T(512)S(1)} fusion(s32[1024]{0:T(1024)S(1)} %bitcast.78, s32[1024]{0:T(1024)S(1)} %reshape.135, s32[]{:T(128)} %constant.12.clone.1), kind=kCustom, calls=%fused_computation.50 | custom fusion | bytes 1032 | tf_op jit(solution)/shard_map/scatter | solution.py:30
  5.4 1.3 concatenate.3
  6.7 1.8 gather_fusion
  8.6 53.6 %all_to_all.10 = bf16[16,16,4096]{2,1,0:T(8,128)(2,1)S(1)} all-to-all(bf16[16,16,4096]{2,1,0:T(8,128)(2,1)S(1)} %bitcast.74), channel_id=1, replica_groups=mesh['groups'=2,'expert'=16] {'expert'}, dimensions={0} | all-to-all | bytes 4194304 | tf_op jit(solution)/shard_map/all_to_all | solution.py:43
  62.1 0.0 copy-start
  62.1 1.3 copy-done
  63.5 6.4 %fusion.4 = f32[256,1536]{1,0:T(8,128)S(1)} fusion(bf16[256,4096]{1,0:T(8,128)(2,1)S(1)} %bitcast.76, bf16[1,4096,1536]{2,1,0:T(8,128)(2,1)} %param.8), kind=kOutput, calls=%fused_computation.14 | convolution fusion | flops 3221225472 | bytes 16252928 | tf_op jit(solution)/shard_map/dot_general | solution.py:11
  69.9 16.8 %fusion.6 = bf16[256,4096]{1,0:T(8,128)(2,1)} fusion(bf16[1,1536,4096]{2,1,0:T(8,128)(2,1)} %param.10, bf16[256,4096]{1,0:T(8,128)(2,1)} %bitcast.77, bf16[1,4096,1536]{2,1,0:T(8,128)(2,1)} %param.9, f32[256,1536]{1,0:T(8,128)S(1)} %fusion.4), kind=kOutput, calls=%fused_computation.16 | convolution fusion | flops 6445858816 | bytes 30932992 | tf_op jit(solution)/shard_map/dot_general | solution.py:14
  86.7 0.0 copy-start.1
  86.7 0.0 copy-start.2
  86.7 5.0 %all-to-all-start.1 = ((bf16[16,16,4096]{2,1,0:T(8,128)(2,1)}), bf16[16,16,4096]{2,1,0:T(8,128)(2,1)S(1)}, u32[]{:S(2)}, u32[]{:S(2)}) async-start(bf16[16,16,4096]{2,1,0:T(8,128)(2,1)} %bitcast.75), calls=%async_computation.1 | async-start | bytes 4194304 | tf_op jit(solution)/shard_map/all_to_all | solution.py:50
  91.8 0.0 copy-done.1
  91.8 0.0 copy-done.2
  91.8 47.5 %all-to-all-done.1 = bf16[16,16,4096]{2,1,0:T(8,128)(2,1)S(1)} async-done(((bf16[16,16,4096]{2,1,0:T(8,128)(2,1)}), bf16[16,16,4096]{2,1,0:T(8,128)(2,1)S(1)}, u32[]{:S(2)}, u32[]{:S(2)}) %all-to-all-start.1) | async-done | bytes 2097184 | tf_op jit(solution)/shard_map/all_to_all | solution.py:50
  139.3 2.6 %bitcast_convert_fusion = f32[256,4096]{1,0:T(8,128)} fusion(bf16[16,16,4096]{2,1,0:T(8,128)(2,1)S(1)} %all-to-all-done.1), kind=kLoop, calls=%fused_computation.19 | loop fusion | flops 1048576 | bytes 6291456 | tf_op jit(solution)/shard_map/reshape | solution.py:59
  141.9 4.4 %gather_fusion.1 = f32[128,4096]{1,0:T(8,128)S(1)} fusion(f32[256,4096]{1,0:T(8,128)} %bitcast_convert_fusion, s32[1024]{0:T(1024)S(1)} %get-tuple-element.36), kind=kCustom, calls=%fused_computation.1 | custom fusion | bytes 4194816 | tf_op jit(solution)/shard_map/gather | solution.py:64
  146.3 5.6 %gather_fusion.2 = f32[128,4096]{1,0:T(8,128)} fusion(f32[256,4096]{1,0:T(8,128)} %bitcast_convert_fusion, s32[1024]{0:T(1024)S(1)} %get-tuple-element.35), kind=kCustom, calls=%fused_computation.2 | custom fusion | bytes 4194816 | tf_op jit(solution)/shard_map/gather | solution.py:64
  152.0 5.6 %gather_fusion.3 = f32[128,4096]{1,0:T(8,128)} fusion(f32[256,4096]{1,0:T(8,128)} %bitcast_convert_fusion, s32[1024]{0:T(1024)S(1)} %get-tuple-element.34), kind=kCustom, calls=%fused_computation.3 | custom fusion | bytes 4194816 | tf_op jit(solution)/shard_map/gather | solution.py:64
  157.6 5.6 %gather_fusion.4 = f32[128,4096]{1,0:T(8,128)} fusion(f32[256,4096]{1,0:T(8,128)} %bitcast_convert_fusion, s32[1024]{0:T(1024)S(1)} %get-tuple-element.33), kind=kCustom, calls=%fused_computation.4 | custom fusion | bytes 4194816 | tf_op jit(solution)/shard_map/gather | solution.py:64
  163.2 5.6 %gather_fusion.5 = f32[128,4096]{1,0:T(8,128)} fusion(f32[256,4096]{1,0:T(8,128)} %bitcast_convert_fusion, s32[1024]{0:T(1024)S(1)} %get-tuple-element.32), kind=kCustom, calls=%fused_computation.5 | custom fusion | bytes 4194816 | tf_op jit(solution)/shard_map/gather | solution.py:64
  168.8 5.7 %gather_fusion.6 = f32[128,4096]{1,0:T(8,128)} fusion(f32[256,4096]{1,0:T(8,128)} %bitcast_convert_fusion, s32[1024]{0:T(1024)S(1)} %get-tuple-element.31), kind=kCustom, calls=%fused_computation.6 | custom fusion | bytes 4194816 | tf_op jit(solution)/shard_map/gather | solution.py:64
  174.5 5.9 %gather_fusion.7 = f32[128,4096]{1,0:T(8,128)} fusion(f32[256,4096]{1,0:T(8,128)} %bitcast_convert_fusion, s32[1024]{0:T(1024)S(1)} %get-tuple-element.30), kind=kCustom, calls=%fused_computation.7 | custom fusion | bytes 4194816 | tf_op jit(solution)/shard_map/gather | solution.py:64
  180.3 5.6 %gather_fusion.8 = f32[128,4096]{1,0:T(8,128)} fusion(f32[256,4096]{1,0:T(8,128)} %bitcast_convert_fusion, s32[1024]{0:T(1024)S(1)} %get-tuple-element.29), kind=kCustom, calls=%fused_computation.8 | custom fusion | bytes 4194816 | tf_op jit(solution)/shard_map/gather | solution.py:64
  186.0 7.4 %add_convert_fusion = bf16[128,4096]{1,0:T(8,128)(2,1)} fusion(f32[128,4096]{1,0:T(8,128)} %gather_fusion.8, f32[128,4096]{1,0:T(8,128)} %gather_fusion.7, f32[128,4096]{1,0:T(8,128)} %gather_fusion.6, f32[128,4096]{1,0:T(8,128)} %gather_fusion.5, f32[128,4096]{1,0:T(8,128)} %gather_fusion.4, f32[128,4096]{1,0:T(8,128)} %gather_fusion.3, ...), kind=kLoop, calls=%fused_computation.20 | loop fusion | flops 12582912 | bytes 17830912 | tf_op jit(solution)/shard_map/convert_element_type | solution.py:66
  (12 shorter events, 0.1 us)
Async XLA Ops:
  62.1 1.3 copy-start
  86.7 5.0 %copy-start.1 = (s32[128,8]{0,1:T(8,128)S(1)}, s32[128,8]{0,1:T(8,128)}, u32[]{:S(2)}) copy-start(s32[128,8]{0,1:T(8,128)} %param.12) | copy-start | bytes 12292
  86.7 5.1 %copy-start.2 = (f32[128,8]{0,1:T(8,128)S(1)}, f32[128,8]{0,1:T(8,128)}, u32[]{:S(2)}) copy-start(f32[128,8]{0,1:T(8,128)} %param.13) | copy-start | bytes 12292
  86.7 52.6 %all-to-all-start.1 = ((bf16[16,16,4096]{2,1,0:T(8,128)(2,1)}), bf16[16,16,4096]{2,1,0:T(8,128)(2,1)S(1)}, u32[]{:S(2)}, u32[]{:S(2)}) async-start(bf16[16,16,4096]{2,1,0:T(8,128)(2,1)} %bitcast.75), calls=%async_computation.1 | async-start | bytes 4194304 | tf_op jit(solution)/shard_map/all_to_all | solution.py:50
where the time goes:
time: 194 us; the launch traced here: 193 us
  blocking collectives  53.6 us (28%)
  local copies, waits for them, and re-layouts  53.2 us (27%)
  waiting for transfers between devices  47.5 us (24%)
  matrix products  23.2 us (12%)
  other arithmetic  10.8 us (6%)
  starting transfers between devices  4.97 us (3%)
    all_to_all x1, blocking collectives, body(): lax.all_to_all(jnp.repeat(outgoing, shards, axis=0), 'expert', split_axis...  53.6 us
    all_to_all x1, waiting for transfers between devices, body(): lax.all_to_all(partial_value.reshape(devices, CAP, model_width), 'expert'...  47.5 us
    gather x8, local copies, waits for them, and re-layouts, body(): expert_out[picked]  44 us
    dot_general x1, matrix products, swiglu_rows(): return jnp.dot(hidden, down_weight[0], preferred_element_type=jnp.float32)  16.8 us
    convert_element_type x1, other arithmetic, body(): return combined.astype(jnp.bfloat16)  7.45 us
    dot_general x1, matrix products, swiglu_rows(): jnp.dot(slot_rows, gate_weight[0], preferred_element_type=jnp.float32)  6.43 us
    all_to_all x1, starting transfers between devices, body(): lax.all_to_all(partial_value.reshape(devices, CAP, model_width), 'expert'...  4.97 us
    scatter x1, local copies, waits for them, and re-layouts, body(): source_row = jnp.full((region + 1,), token_count, jnp.int32).at[target.re...  4.3 us
  transfers between devices with their start and end apart: 1, of which 1 were waited for; matrix products, arithmetic and copies ran while one was open for 0% of the time, Pallas kernels for 0%

commit v1 on v0

v1 whole, which is shorter than its diff:
```python
import functools

import jax
import jax.numpy as jnp
from jax import lax
from jax.experimental import pallas as pl
from jax.experimental.pallas import tpu as pltpu
from jax.sharding import PartitionSpec as P

EXPERTS = 16
CAP = 16
GROUPS = 4
ORDER = (2, 3, 1, 0)


def xor_index(a, b, n):
    out, bit = 0, 1
    while bit < n:
        out = out + ((a // bit + b // bit) % 2) * bit
        bit *= 2
    return out


def column_tile(width, most):
    tile = most
    while width % tile:
        tile //= 2
    return tile


def kernel(
    n, tokens_ref, ids_ref, slots_ref, gates_ref, gate_hbm, up_hbm, down_hbm, out_ref,
    gate_w, up_w, down_w, send, inbox, outbox, back, hidden, acc, pack, weight_sems,
    there_send, there_recv, back_send, back_recv,
):
    me = lax.axis_index("expert")
    shards = n // EXPERTS
    per_group = n // GROUPS
    rows = per_group * CAP
    token_count, width = tokens_ref.shape
    ff = gate_w.shape[1]
    top = ids_ref.shape[1]

    weights = [
        pltpu.make_async_copy(src.at[0], dst, weight_sems.at[i])
        for i, (src, dst) in enumerate(((gate_hbm, gate_w), (up_hbm, up_w), (down_hbm, down_w)))
    ]
    for copy in weights:
        copy.start()

    barrier = pltpu.get_barrier_semaphore()

    def greet(j, carry):
        pl.semaphore_signal(barrier, inc=1, device_id={"expert": xor_index(me, j, n)})
        return carry

    lax.fori_loop(1, n, greet, 0)

    target = jnp.where(slots_ref[...] >= 0, ids_ref[...] * CAP + slots_ref[...], -1)
    lane = lax.broadcasted_iota(jnp.int32, (token_count, EXPERTS * CAP), 1)
    chosen = jnp.zeros((token_count, EXPERTS * CAP), jnp.float32)
    for k in range(top):
        chosen = jnp.where(target[:, k : k + 1] == lane, 1.0, chosen)
    pack[...] = chosen.T.astype(jnp.bfloat16)
    tile_p = column_tile(width, 512)

    def pack_tile(i, carry):
        cols = pl.ds(pl.multiple_of(i * tile_p, tile_p), tile_p)
        send[:, cols] = jnp.dot(
            pack[...], tokens_ref[:, cols], preferred_element_type=jnp.float32
        ).astype(jnp.bfloat16)
        return carry

    lax.fori_loop(0, width // tile_p, pack_tile, 0)
    pl.semaphore_wait(barrier, n - 1)

    def block(j):
        return pl.ds(pl.multiple_of(j * CAP, CAP), CAP)

    def dispatch(j):
        peer = xor_index(me, j, n)
        return pltpu.make_async_remote_copy(
            src_ref=send.at[block(peer // shards)],
            dst_ref=inbox.at[block(j)],
            send_sem=there_send.at[j],
            recv_sem=there_recv.at[j],
            device_id={"expert": peer},
        )

    def giveback(j):
        return pltpu.make_async_remote_copy(
            src_ref=outbox.at[block(j)],
            dst_ref=back.at[block(j)],
            send_sem=back_send.at[j],
            recv_sem=back_recv.at[j],
            device_id={"expert": xor_index(me, j, n)},
        )

    def each(group, act):
        first = max(group * per_group, 1)

        def step(j, carry):
            act(j)
            return carry

        lax.fori_loop(first, (group + 1) * per_group, step, 0)

    for group in ORDER:
        each(group, lambda j: dispatch(j).start())
    inbox[0:CAP, :] = send[block(me // shards), :]

    tile_f = column_tile(ff, 256)
    tile_d = column_tile(width, 512)
    for place, group in enumerate(ORDER):
        mine = slice(group * rows, (group + 1) * rows)
        each(group, lambda j: dispatch(j).wait_recv())
        if place == 0:
            weights[0].wait()
            weights[1].wait()

        def first_half(i, carry):
            cols = pl.ds(pl.multiple_of(i * tile_f, tile_f), tile_f)
            gate_val = jnp.dot(
                inbox[mine, :], gate_w[:, cols], preferred_element_type=jnp.float32
            )
            up_val = jnp.dot(inbox[mine, :], up_w[:, cols], preferred_element_type=jnp.float32)
            hidden[:, cols] = (jax.nn.silu(gate_val) * up_val).astype(jnp.bfloat16)
            return carry

        lax.fori_loop(0, ff // tile_f, first_half, 0)
        if place == 0:
            weights[2].wait()

        def second_half(i, carry):
            cols = pl.ds(pl.multiple_of(i * tile_d, tile_d), tile_d)
            outbox[mine, cols] = jnp.dot(
                hidden[...], down_w[:, cols], preferred_element_type=jnp.float32
            ).astype(jnp.bfloat16)
            return carry

        lax.fori_loop(0, width // tile_d, second_half, 0)
        each(group, lambda j: giveback(j).start())
    back[0:CAP, :] = outbox[0:CAP, :]

    def mix_group(place, group):
        mine = slice(group * rows, (group + 1) * rows)
        column = lax.broadcasted_iota(jnp.int32, (token_count, rows), 1) + group * rows
        expert = ((column // CAP) ^ me) // shards
        key = expert * CAP + column % CAP
        mix = jnp.zeros((token_count, rows), jnp.float32)
        for k in range(top):
            mix = jnp.where(target[:, k : k + 1] == key, gates_ref[:, k : k + 1], mix)
        high = mix.astype(jnp.bfloat16)
        low = (mix - high.astype(jnp.float32)).astype(jnp.bfloat16)
        both = jnp.concatenate([high, low], axis=0)
        each(group, lambda j: giveback(j).wait_recv())

        def mix_tile(i, carry):
            cols = pl.ds(pl.multiple_of(i * tile_d, tile_d), tile_d)
            product = jnp.dot(both, back[mine, cols], preferred_element_type=jnp.float32)
            total = product[:token_count] + product[token_count:]
            if place > 0:
                total = total + acc[:, cols]
            if place < GROUPS - 1:
                acc[:, cols] = total
            else:
                out_ref[:, cols] = total.astype(jnp.bfloat16)
            return carry

        lax.fori_loop(0, width // tile_d, mix_tile, 0)

    for place, group in enumerate((0, 1, 2, 3)):
        mix_group(place, group)
    for group in range(GROUPS):
        each(group, lambda j: dispatch(j).wait_send())
        each(group, lambda j: giveback(j).wait_send())


def body(tokens, gate_weight, up_weight, down_weight, expert_ids, slots, gates):
    n = lax.axis_size("expert")
    token_count, width = tokens.shape
    ff = gate_weight.shape[2]
    rows = n // GROUPS * CAP
    vmem = pl.BlockSpec(memory_space=pltpu.VMEM)
    hbm = pl.BlockSpec(memory_space=pl.ANY)
    return pl.pallas_call(
        functools.partial(kernel, n),
        out_shape=jax.ShapeDtypeStruct((token_count, width), jnp.bfloat16),
        in_specs=[vmem] * 4 + [hbm] * 3,
        out_specs=vmem,
        scratch_shapes=[
            pltpu.VMEM((width, ff), jnp.bfloat16),
            pltpu.VMEM((width, ff), jnp.bfloat16),
            pltpu.VMEM((ff, width), jnp.bfloat16),
            pltpu.VMEM((EXPERTS * CAP, width), jnp.bfloat16),
            pltpu.VMEM((n * CAP, width), jnp.bfloat16),
            pltpu.VMEM((n * CAP, width), jnp.bfloat16),
            pltpu.VMEM((n * CAP, width), jnp.bfloat16),
            pltpu.VMEM((rows, ff), jnp.bfloat16),
            pltpu.VMEM((token_count, width), jnp.float32),
            pltpu.VMEM((EXPERTS * CAP, token_count), jnp.bfloat16),
            pltpu.SemaphoreType.DMA((3,)),
            pltpu.SemaphoreType.DMA((n,)),
            pltpu.SemaphoreType.DMA((n,)),
            pltpu.SemaphoreType.DMA((n,)),
            pltpu.SemaphoreType.DMA((n,)),
        ],
        compiler_params=pltpu.CompilerParams(
            collective_id=0, has_side_effects=True, vmem_limit_bytes=58 * 1024 * 1024
        ),
        name="expert_layer",
    )(tokens, expert_ids, slots, gates, gate_weight, up_weight, down_weight)


def solution(mesh):
    return jax.shard_map(
        body,
        mesh=mesh,
        in_specs=(
            P(("groups", "expert"), None),
            P("expert", None, None),
            P("expert", None, None),
            P("expert", None, None),
            P(("groups", "expert"), None),
            P(("groups", "expert"), None),
            P(("groups", "expert"), None),
        ),
        out_specs=P(("groups", "expert"), None),
        check_vma=False,
    )
```

time: 194 us -> 120 us (0.62)
  Pallas kernels: 0 us -> 113 us
  blocking collectives: 53.6 us -> 0 us
  waiting for transfers between devices: 47.5 us -> 0 us
  local copies, waits for them, and re-layouts: 53.2 us -> 6.51 us
  matrix products: 23.2 us -> 0 us
  other arithmetic: 10.8 us -> 0 us
  starting transfers between devices: 4.97 us -> 0 us
    pallas_call x0 -> x1, Pallas kernels: none -> 113 us  [body(): pl.pallas_call(functools.partial(kernel, n), out_shape=jax.ShapeDtypeStru...]
    all_to_all x1 -> x0, blocking collectives: 53.6 us -> none  [body(): lax.all_to_all(jnp.repeat(outgoing, shards, axis=0), 'expert', split_axis...]
    all_to_all x1 -> x0, waiting for transfers between devices: 47.5 us -> none  [body(): lax.all_to_all(partial_value.reshape(devices, CAP, model_width), 'expert'...]
    gather x9 -> x0, local copies, waits for them, and re-layouts: 45.9 us -> none  [the longest x8 44 us: body(): expert_out[picked]]
    dot_general x2 -> x0, matrix products: 23.2 us -> none  [the longest x1 16.8 us: swiglu_rows(): return jnp.dot(hidden, down_weight[0], preferred_element_type=jnp.float32)]
    convert_element_type x1 -> x0, other arithmetic: 7.45 us -> none  [body(): return combined.astype(jnp.bfloat16)]
    unnamed x6 -> x4, local copies, waits for them, and re-layouts: 1.34 us -> 6.51 us
    all_to_all x1 -> x0, starting transfers between devices: 4.97 us -> none  [body(): lax.all_to_all(partial_value.reshape(devices, CAP, model_width), 'expert'...]
  transfers between devices with their start and end apart: 1 -> 0, of which waited for: 1 -> 0; matrix products, arithmetic and copies ran while one was open for 0% -> 0% of each run, Pallas kernels for 0% -> 0%
where the time goes in v1:
time: 120 us
  Pallas kernels  113 us (94%)
  local copies, waits for them, and re-layouts  6.51 us (5%)
    pallas_call x1, Pallas kernels, body(): pl.pallas_call(functools.partial(kernel, n), out_shape=jax.ShapeDtypeStru...  113 us
    unnamed x4, local copies, waits for them, and re-layouts  6.51 us

profile of v1, /device:TPU:16, one launch (start us, length us, event | category | flops | bytes accessed | tf_op | source)
XLA Modules:
  0.0 120.0 jit_solution(4668551798306926157)
XLA Ops:
  0.0 1.4 %copy.8.ids_ref = s32[128,8]{1,0:T(8,128)} copy(s32[128,8]{0,1:T(8,128)} %param.11) | data formatting | bytes 8192 | tf_op args[4]
  1.4 1.4 %copy.9.slots_ref = s32[128,8]{1,0:T(8,128)} copy(s32[128,8]{0,1:T(8,128)} %param.12) | data formatting | bytes 8192 | tf_op args[5]
  2.8 1.4 %copy.10.gates_ref = f32[128,8]{1,0:T(8,128)} copy(f32[128,8]{0,1:T(8,128)} %param.13) | data formatting | bytes 8192 | tf_op args[6]
  4.2 113.5 %expert_layer.1 = bf16[128,4096]{1,0:T(8,128)(2,1)} custom-call(bf16[128,4096]{1,0:T(8,128)(2,1)} %tokens_ref.1, s32[128,8]{1,0:T(8,128)} %copy.8.ids_ref, s32[128,8]{1,0:T(8,128)} %copy.9.slots_ref, f32[128,8]{1,0:T(8,128)} %copy.10.gates_ref, bf16[1,4096,1536]{2,1,0:T(8,128)(2,1)} %gate_hbm.1, bf16[1,4096,1536]{2,1,0:T(8,128)(2,1)} %up_hbm.1, ...), custom_call_target="tpu_custom_call" | custom-call | tf_op jit(solution)/shard_map/expert_layer/pallas_call | solution.py:186
  117.7 2.3 %copy.12 = bf16[128,4096]{1,0:T(8,128)(2,1)} copy(bf16[128,4096]{1,0:T(8,128)(2,1)} %expert_layer.1) | data formatting | bytes 2097152

commit v2 on v1

--- a/solution.py
+++ b/solution.py
@@ -9,8 +9,9 @@
 
 EXPERTS = 16
 CAP = 16
-GROUPS = 4
-ORDER = (2, 3, 1, 0)
+SENDS = ((8, 8), (4, 4), (0, 4))
+WORKS = ((8, 4), (0, 8), (12, 2), (14, 2))
+MIXES = ((0, 8), (8, 4), (12, 4))
 
 
 def xor_index(a, b, n):
@@ -35,11 +36,10 @@
 ):
     me = lax.axis_index("expert")
     shards = n // EXPERTS
-    per_group = n // GROUPS
-    rows = per_group * CAP
+    unit = n // EXPERTS
     token_count, width = tokens_ref.shape
     ff = gate_w.shape[1]
-    top = ids_ref.shape[1]
+    top = ids_ref.shape[0]
 
     weights = [
         pltpu.make_async_copy(src.at[0], dst, weight_sems.at[i])
@@ -57,11 +57,11 @@
     lax.fori_loop(1, n, greet, 0)
 
     target = jnp.where(slots_ref[...] >= 0, ids_ref[...] * CAP + slots_ref[...], -1)
-    lane = lax.broadcasted_iota(jnp.int32, (token_count, EXPERTS * CAP), 1)
-    chosen = jnp.zeros((token_count, EXPERTS * CAP), jnp.float32)
+    slot_row = lax.broadcasted_iota(jnp.int32, (EXPERTS * CAP, token_count), 0)
+    chosen = jnp.zeros((EXPERTS * CAP, token_count), jnp.float32)
     for k in range(top):
-        chosen = jnp.where(target[:, k : k + 1] == lane, 1.0, chosen)
-    pack[...] = chosen.T.astype(jnp.bfloat16)
+        chosen = jnp.where(target[k : k + 1, :] == slot_row, 1.0, chosen)
+    pack[...] = chosen.astype(jnp.bfloat16)
     tile_p = column_tile(width, 512)
 
     def pack_tile(i, carry):
@@ -97,22 +97,23 @@
         )
 
     def each(group, act):
-        first = max(group * per_group, 1)
+        first, count = group[0] * unit, group[1] * unit
 
         def step(j, carry):
             act(j)
             return carry
 
-        lax.fori_loop(first, (group + 1) * per_group, step, 0)
-
-    for group in ORDER:
+        lax.fori_loop(max(first, 1), first + count, step, 0)
+
+    for group in SENDS:
         each(group, lambda j: dispatch(j).start())
     inbox[0:CAP, :] = send[block(me // shards), :]
 
     tile_f = column_tile(ff, 256)
     tile_d = column_tile(width, 512)
-    for place, group in enumerate(ORDER):
-        mine = slice(group * rows, (group + 1) * rows)
+    for place, group in enumerate(WORKS):
+        start, rows = group[0] * unit * CAP, group[1] * unit * CAP
+        mine = slice(start, start + rows)
         each(group, lambda j: dispatch(j).wait_recv())
         if place == 0:
             weights[0].wait()
@@ -124,7 +125,7 @@
                 inbox[mine, :], gate_w[:, cols], preferred_element_type=jnp.float32
             )
             up_val = jnp.dot(inbox[mine, :], up_w[:, cols], preferred_element_type=jnp.float32)
-            hidden[:, cols] = (jax.nn.silu(gate_val) * up_val).astype(jnp.bfloat16)
+            hidden[:rows, cols] = (jax.nn.silu(gate_val) * up_val).astype(jnp.bfloat16)
             return carry
 
         lax.fori_loop(0, ff // tile_f, first_half, 0)
@@ -134,7 +135,7 @@
         def second_half(i, carry):
             cols = pl.ds(pl.multiple_of(i * tile_d, tile_d), tile_d)
             outbox[mine, cols] = jnp.dot(
-                hidden[...], down_w[:, cols], preferred_element_type=jnp.float32
+                hidden[:rows, :], down_w[:, cols], preferred_element_type=jnp.float32
             ).astype(jnp.bfloat16)
             return carry
 
@@ -143,13 +144,15 @@
     back[0:CAP, :] = outbox[0:CAP, :]
 
     def mix_group(place, group):
-        mine = slice(group * rows, (group + 1) * rows)
-        column = lax.broadcasted_iota(jnp.int32, (token_count, rows), 1) + group * rows
-        expert = ((column // CAP) ^ me) // shards
-        key = expert * CAP + column % CAP
-        mix = jnp.zeros((token_count, rows), jnp.float32)
+        start, rows = group[0] * unit * CAP, group[1] * unit * CAP
+        mine = slice(start, start + rows)
+        row = lax.broadcasted_iota(jnp.int32, (rows, token_count), 0) + start
+        expert = ((row // CAP) ^ me) // shards
+        key = expert * CAP + row % CAP
+        mix = jnp.zeros((rows, token_count), jnp.float32)
         for k in range(top):
-            mix = jnp.where(target[:, k : k + 1] == key, gates_ref[:, k : k + 1], mix)
+            mix = jnp.where(target[k : k + 1, :] == key, gates_ref[k : k + 1, :], mix)
+        mix = mix.T
         high = mix.astype(jnp.bfloat16)
         low = (mix - high.astype(jnp.float32)).astype(jnp.bfloat16)
         both = jnp.concatenate([high, low], axis=0)
@@ -161,7 +164,7 @@
             total = product[:token_count] + product[token_count:]
             if place > 0:
                 total = total + acc[:, cols]
-            if place < GROUPS - 1:
+            if place < len(MIXES) - 1:
                 acc[:, cols] = total
             else:
                 out_ref[:, cols] = total.astype(jnp.bfloat16)
@@ -169,18 +172,17 @@
 
         lax.fori_loop(0, width // tile_d, mix_tile, 0)
 
-    for place, group in enumerate((0, 1, 2, 3)):
+    for place, group in enumerate(MIXES):
         mix_group(place, group)
-    for group in range(GROUPS):
-        each(group, lambda j: dispatch(j).wait_send())
-        each(group, lambda j: giveback(j).wait_send())
+    each((0, EXPERTS), lambda j: dispatch(j).wait_send())
+    each((0, EXPERTS), lambda j: giveback(j).wait_send())
 
 
 def body(tokens, gate_weight, up_weight, down_weight, expert_ids, slots, gates):
     n = lax.axis_size("expert")
     token_count, width = tokens.shape
     ff = gate_weight.shape[2]
-    rows = n // GROUPS * CAP
+    rows = max(count for _, count in WORKS) * (n // EXPERTS) * CAP
     vmem = pl.BlockSpec(memory_space=pltpu.VMEM)
     hbm = pl.BlockSpec(memory_space=pl.ANY)
     return pl.pallas_call(
@@ -209,7 +211,7 @@
             collective_id=0, has_side_effects=True, vmem_limit_bytes=58 * 1024 * 1024
         ),
         name="expert_layer",
-    )(tokens, expert_ids, slots, gates, gate_weight, up_weight, down_weight)
+    )(tokens, expert_ids.T, slots.T, gates.T, gate_weight, up_weight, down_weight)
 
 
 def solution(mesh):

time: 120 us -> 102 us (0.85)
  Pallas kernels: 113 us -> 99.1 us
  local copies, waits for them, and re-layouts: 6.51 us -> 2.29 us
    pallas_call x1, Pallas kernels: 113 us -> 99.1 us  [body(): pl.pallas_call(functools.partial(kernel, n), out_shape=jax.ShapeDtypeStru...]
    unnamed x4 -> x1, local copies, waits for them, and re-layouts: 6.51 us -> 2.29 us
where the time goes in v2:
time: 102 us; the launch traced here: 101 us
  Pallas kernels  99.1 us (97%)
  local copies, waits for them, and re-layouts  2.29 us (2%)
    pallas_call x1, Pallas kernels, body(): pl.pallas_call(functools.partial(kernel, n), out_shape=jax.ShapeDtypeStru...  99.1 us
    unnamed x1, local copies, waits for them, and re-layouts  2.29 us

profile of v2, /device:TPU:16, one launch (start us, length us, event | category | flops | bytes accessed | tf_op | source)
XLA Modules:
  0.0 101.4 jit_solution(12391783972465603229)
XLA Ops:
  0.0 99.1 %expert_layer.1 = bf16[128,4096]{1,0:T(8,128)(2,1)} custom-call(bf16[128,4096]{1,0:T(8,128)(2,1)} %tokens_ref.1, s32[8,128]{1,0:T(8,128)} %bitcast.3, s32[8,128]{1,0:T(8,128)} %bitcast.4, f32[8,128]{1,0:T(8,128)} %bitcast.5, bf16[1,4096,1536]{2,1,0:T(8,128)(2,1)} %gate_hbm.1, bf16[1,4096,1536]{2,1,0:T(8,128)(2,1)} %up_hbm.1, bf16[1,1536,4096]{2,1,0:T(8,128)(2,1)} %down_hbm.1), custom_call_target="tpu_custom_call" | custom-call | tf_op jit(solution)/shard_map/expert_layer/pallas_call | solution.py:188
  99.2 2.3 %copy.9 = bf16[128,4096]{1,0:T(8,128)(2,1)} copy(bf16[128,4096]{1,0:T(8,128)(2,1)} %expert_layer.1) | data formatting | bytes 2097152

commit v3 on v2

--- a/solution.py
+++ b/solution.py
@@ -187,7 +187,7 @@
     hbm = pl.BlockSpec(memory_space=pl.ANY)
     return pl.pallas_call(
         functools.partial(kernel, n),
-        out_shape=jax.ShapeDtypeStruct((token_count, width), jnp.bfloat16),
+        out_shape=pltpu.VMEM((token_count, width), jnp.bfloat16),
         in_specs=[vmem] * 4 + [hbm] * 3,
         out_specs=vmem,
         scratch_shapes=[

time: 102 us -> 100 us (0.980)
  local copies, waits for them, and re-layouts: 2.29 us -> 0.97 us
    unnamed x1, local copies, waits for them, and re-layouts: 2.29 us -> 0.97 us
where the time goes in v3:
time: 100 us; the launch traced here: 99.1 us
  Pallas kernels  98.1 us (98%)
    pallas_call x1, Pallas kernels, body(): pl.pallas_call(functools.partial(kernel, n), out_shape=pltpu.VMEM((token_...  98.1 us

profile of v3, /device:TPU:16, one launch (start us, length us, event | category | flops | bytes accessed | tf_op | source)
XLA Modules:
  0.0 99.1 jit_solution(3906636739755415904)
XLA Ops:
  0.0 98.1 %expert_layer.1 = bf16[128,4096]{1,0:T(8,128)(2,1)S(1)} custom-call(bf16[128,4096]{1,0:T(8,128)(2,1)} %tokens_ref.1, s32[8,128]{1,0:T(8,128)} %bitcast.3, s32[8,128]{1,0:T(8,128)} %bitcast.4, f32[8,128]{1,0:T(8,128)} %bitcast.5, bf16[1,4096,1536]{2,1,0:T(8,128)(2,1)} %gate_hbm.1, bf16[1,4096,1536]{2,1,0:T(8,128)(2,1)} %up_hbm.1, bf16[1,1536,4096]{2,1,0:T(8,128)(2,1)} %down_hbm.1), custom_call_target="tpu_custom_call" | custom-call | tf_op jit(solution)/shard_map/expert_layer/pallas_call | solution.py:188
  98.2 1.0 copy.9

commit v4 on v3

--- a/solution.py
+++ b/solution.py
@@ -9,7 +9,7 @@
 
 EXPERTS = 16
 CAP = 16
-SENDS = ((8, 8), (4, 4), (0, 4))
+SENDS = ((8, 8), (0, 4), (4, 4))
 WORKS = ((8, 4), (0, 8), (12, 2), (14, 2))
 MIXES = ((0, 8), (8, 4), (12, 4))
 
@@ -45,8 +45,6 @@
         pltpu.make_async_copy(src.at[0], dst, weight_sems.at[i])
         for i, (src, dst) in enumerate(((gate_hbm, gate_w), (up_hbm, up_w), (down_hbm, down_w)))
     ]
-    for copy in weights:
-        copy.start()
 
     barrier = pltpu.get_barrier_semaphore()
 
@@ -107,6 +105,8 @@
 
     for group in SENDS:
         each(group, lambda j: dispatch(j).start())
+    for copy in weights:
+        copy.start()
     inbox[0:CAP, :] = send[block(me // shards), :]
 
     tile_f = column_tile(ff, 256)

time: 100 us -> 99.9 us (level)
  no operation moved by 1% of the time
where the time goes in v4:
time: 99.9 us; the launch traced here: 99.1 us
  Pallas kernels  98.1 us (98%)
    pallas_call x1, Pallas kernels, body(): pl.pallas_call(functools.partial(kernel, n), out_shape=pltpu.VMEM((token_...  98.1 us

profile of v4, /device:TPU:16, one launch (start us, length us, event | category | flops | bytes accessed | tf_op | source)
XLA Modules:
  0.0 99.1 jit_solution(5334831884222870514)
XLA Ops:
  0.0 98.1 %expert_layer.1 = bf16[128,4096]{1,0:T(8,128)(2,1)S(1)} custom-call(bf16[128,4096]{1,0:T(8,128)(2,1)} %tokens_ref.1, s32[8,128]{1,0:T(8,128)} %bitcast.3, s32[8,128]{1,0:T(8,128)} %bitcast.4, f32[8,128]{1,0:T(8,128)} %bitcast.5, bf16[1,4096,1536]{2,1,0:T(8,128)(2,1)} %gate_hbm.1, bf16[1,4096,1536]{2,1,0:T(8,128)(2,1)} %up_hbm.1, bf16[1,1536,4096]{2,1,0:T(8,128)(2,1)} %down_hbm.1), custom_call_target="tpu_custom_call" | custom-call | tf_op jit(solution)/shard_map/expert_layer/pallas_call | solution.py:188
  98.1 1.0 copy.9
